TPU v7x, 32 devices: a whole 2x2x4 slice. The times are simulated.
32 devices in a mesh: dp: 16 (over z, y, core), mp: 2 (over x).
Axes of the slice: x: 2, y: 2, z: 4, core: 2. Of those that a mesh axis runs over, the one named last changes fastest.
Arguments:
- tokens_in: bfloat16 [32768, 768], P(('dp', 'mp')), may hold values from -6 to 6
- seg_lengths: int32 [64, 4], P('dp'), may hold values from 1 to 256, 512 in all within a row
- pad_counts: int32 [64], P('dp'), may hold values from 0 to 64
- w_qkv: bfloat16 [3, 768, 768], P(None, None, 'mp'), may hold values from -0.21875 to 0.21875
- qv_bias: bfloat16 [2, 768], P(None, 'mp'), may hold values from -3 to 3
- w_out: bfloat16 [768, 768], P('mp'), may hold values from -1.5 to 1.5
- out_bias: bfloat16 [768], replicated, may hold values from -3 to 3
- norm1_gain: bfloat16 [768], replicated, may hold values from 0.5 to 1.5
- norm1_bias: bfloat16 [768], replicated, may hold values from -3 to 3
- w_up: bfloat16 [768, 3072], P(None, 'mp'), may hold values from -0.21875 to 0.21875
- up_bias: bfloat16 [3072], P('mp'), may hold values from -3 to 3
- w_down: bfloat16 [3072, 768], P('mp'), may hold values from -0.109375 to 0.109375
- down_bias: bfloat16 [768], replicated, may hold values from -3 to 3
- norm2_gain: bfloat16 [768], replicated, may hold values from 0.5 to 1.5
- norm2_bias: bfloat16 [768], replicated, may hold values from -3 to 3
- cotangent: bfloat16 [32768, 768], P(('dp', 'mp')), may hold values from -6 to 6
Outputs:
- tokens_out: bfloat16 [32768, 768], P(('dp', 'mp'))
- pooled: float32 [64, 768], P(('dp', 'mp'))
- grad_input: bfloat16 [32768, 768], P(('dp', 'mp'))
- grad_qkv: float32 [3, 768, 768], P(None, None, 'mp')
- grad_qv_bias: float32 [2, 768], P(None, 'mp')
- grad_out: float32 [768, 768], P('mp')
- grad_out_bias: float32 [768], replicated
- grad_norm1_gain: float32 [768], replicated
- grad_norm1_bias: float32 [768], replicated
- grad_up: float32 [768, 3072], P(None, 'mp')
- grad_up_bias: float32 [3072], P('mp')
- grad_down: float32 [3072, 768], P('mp')
- grad_down_bias: float32 [768], replicated
- grad_norm2_gain: float32 [768], replicated
- grad_norm2_bias: float32 [768], replicated
All inputs are finite; a program needn't handle non-finite values.
Results may differ from a plain program's by a relative error of at most 0.019.
Values may be sent and summed in bfloat16 or wider, within the bound.
No kernel may reach another device: no remote copies, remote signals or barrier semaphores. Data moves between devices by JAX's collectives and lax.ppermute only.
A program may use at most 192 MiB of HBM per device.

v0:
```python
import jax
import jax.numpy as jnp
from jax import lax
from jax.sharding import PartitionSpec as P

HD = 64
SEQ = 512


EPSILON = 1e-12
SCORE_SCALE = 0.125
GELU_COEF = 0.7978845608028654


def layer_norm(hidden, gain_vec, shift_vec):
    centered = hidden - jnp.mean(hidden, axis=-1, keepdims=True)
    spread = jnp.mean(centered * centered, axis=-1, keepdims=True)
    return centered * lax.rsqrt(spread + EPSILON) * gain_vec + shift_vec


def gelu_tanh(inputs):
    return (
        0.5 * inputs * (1.0 + jnp.tanh(GELU_COEF * (inputs + 0.044715 * inputs * inputs * inputs)))
    )


def allowed_mask(seg_row, pad_row, seq_len):
    positions = jnp.arange(seq_len, dtype=jnp.int32)
    seg_ends = jnp.cumsum(seg_row)
    segment = jnp.sum((positions[:, None] >= seg_ends[None, :]).astype(jnp.int32), axis=1)
    usable = positions < seq_len - pad_row
    same_doc = segment[:, None] == segment[None, :]
    return same_doc & (usable[None, :] | (positions[:, None] == positions[None, :]))


def attend_row(queries, key_rows, values, allowed):
    scores = jnp.einsum("qhd,khd->hqk", queries, key_rows, preferred_element_type=jnp.float32)
    scaled = jnp.where(allowed[None], scores * SCORE_SCALE, -1e30)
    row_peak = jnp.max(scaled, axis=-1, keepdims=True)
    row_exp = jnp.exp(scaled - row_peak)
    row_total = jnp.sum(row_exp, axis=-1, keepdims=True)
    probs_b = (row_exp / row_total).astype(jnp.bfloat16)
    context = jnp.einsum("hqk,khd->qhd", probs_b, values, preferred_element_type=jnp.float32)
    return (context.astype(jnp.bfloat16), (row_peak + jnp.log(row_total))[..., 0])


def attend_back(queries, key_rows, values, allowed, log_total, grad_ctx):
    scores = jnp.einsum("qhd,khd->hqk", queries, key_rows, preferred_element_type=jnp.float32)
    scaled = jnp.where(allowed[None], scores * SCORE_SCALE, -1e30)
    probs = jnp.exp(scaled - log_total[..., None])
    grad_probs = jnp.einsum("qhd,khd->hqk", grad_ctx, values, preferred_element_type=jnp.float32)
    inner = jnp.sum(probs * grad_probs, axis=-1, keepdims=True)
    grad_scores = (probs * (grad_probs - inner) * SCORE_SCALE).astype(jnp.bfloat16)
    grad_queries = jnp.einsum(
        "hqk,khd->qhd", grad_scores, key_rows, preferred_element_type=jnp.float32
    )
    grad_keys = jnp.einsum("hqk,qhd->khd", grad_scores, queries, preferred_element_type=jnp.float32)
    grad_values = jnp.einsum(
        "hqk,qhd->khd", probs.astype(jnp.bfloat16), grad_ctx, preferred_element_type=jnp.float32
    )
    return (
        grad_queries.astype(jnp.bfloat16),
        grad_keys.astype(jnp.bfloat16),
        grad_values.astype(jnp.bfloat16),
    )


def shards(
    tokens_in,
    seg_lengths,
    pad_counts,
    w_qkv,
    qv_bias,
    w_out,
    out_bias,
    norm1_gain,
    norm1_bias,
    w_up,
    up_bias,
    w_down,
    down_bias,
    norm2_gain,
    norm2_bias,
    cotangent,
):
    rows_here = seg_lengths.shape[0]
    model_width = tokens_in.shape[1]
    local_width = w_qkv.shape[2]
    heads_here = local_width // HD
    row_masks = jax.vmap(allowed_mask, in_axes=(0, 0, None))(seg_lengths, pad_counts, SEQ)
    gain_one = norm1_gain.astype(jnp.float32)
    shift_one = norm1_bias.astype(jnp.float32)
    gain_two = norm2_gain.astype(jnp.float32)
    shift_two = norm2_bias.astype(jnp.float32)
    gathered = lax.all_gather(tokens_in, "mp", axis=0, tiled=True)
    projected = jnp.einsum("td,cde->cte", gathered, w_qkv, preferred_element_type=jnp.float32)
    zero_bias = jnp.zeros((local_width,), jnp.float32)
    bias_stack = jnp.stack(
        [qv_bias[0].astype(jnp.float32), zero_bias, qv_bias[1].astype(jnp.float32)]
    )
    qkv = (
        (projected + bias_stack[:, None, :])
        .astype(jnp.bfloat16)
        .reshape(3, rows_here, SEQ, heads_here, HD)
    )

    def forward_row(row_items):
        return attend_row(row_items[0], row_items[1], row_items[2], row_items[3])

    context, log_total = lax.map(forward_row, (qkv[0], qkv[1], qkv[2], row_masks))
    context = context.reshape(rows_here * SEQ, local_width)
    attended = lax.psum_scatter(
        jnp.dot(context, w_out, preferred_element_type=jnp.float32),
        "mp",
        scatter_dimension=0,
        tiled=True,
    ) + out_bias.astype(jnp.float32)
    residual = tokens_in.astype(jnp.float32) + attended
    normed, norm1_pull = jax.vjp(layer_norm, residual, gain_one, shift_one)
    mid_rows = lax.all_gather(normed.astype(jnp.bfloat16), "mp", axis=0, tiled=True)
    pre_act = jnp.dot(mid_rows, w_up, preferred_element_type=jnp.float32) + up_bias.astype(
        jnp.float32
    )
    activated = gelu_tanh(pre_act).astype(jnp.bfloat16)
    second = (
        normed
        + lax.psum_scatter(
            jnp.dot(activated, w_down, preferred_element_type=jnp.float32).astype(jnp.bfloat16),
            "mp",
            scatter_dimension=0,
            tiled=True,
        ).astype(jnp.float32)
        + down_bias.astype(jnp.float32)
    )
    final_rows, norm2_pull = jax.vjp(layer_norm, second, gain_two, shift_two)
    tokens_out = final_rows.astype(jnp.bfloat16)
    local_count = rows_here // lax.axis_size("mp")
    pad_local = lax.dynamic_slice_in_dim(
        pad_counts, lax.axis_index("mp") * local_count, local_count, 0
    )
    positions = jnp.arange(SEQ, dtype=jnp.int32)
    usable = (positions[None, :] < SEQ - pad_local[:, None]).astype(jnp.float32)
    pooled = (
        jnp.sum(final_rows.reshape(local_count, SEQ, model_width) * usable[..., None], axis=1)
        / (SEQ - pad_local).astype(jnp.float32)[:, None]
    )
    grad_second, grad_gain_two, grad_shift_two = norm2_pull(cotangent.astype(jnp.float32))
    grad_branch = grad_second.astype(jnp.bfloat16)
    grad_down_bias = jnp.sum(grad_branch.astype(jnp.float32), axis=0)
    grad_branch_rows = lax.all_gather(grad_branch, "mp", axis=0, tiled=True)
    grad_down = jnp.einsum(
        "tf,td->fd", activated, grad_branch_rows, preferred_element_type=jnp.float32
    )
    grad_activ = jnp.einsum(
        "td,fd->tf", grad_branch_rows, w_down, preferred_element_type=jnp.float32
    )
    gelu_pull = jax.vjp(gelu_tanh, pre_act)[1]
    grad_upper = gelu_pull(grad_activ)[0].astype(jnp.bfloat16)
    grad_up_bias = jnp.sum(grad_upper.astype(jnp.float32), axis=0)
    grad_up = jnp.einsum("td,tf->df", mid_rows, grad_upper, preferred_element_type=jnp.float32)
    grad_normed = grad_second + lax.psum_scatter(
        jnp.einsum("tf,df->td", grad_upper, w_up, preferred_element_type=jnp.float32).astype(
            jnp.bfloat16
        ),
        "mp",
        scatter_dimension=0,
        tiled=True,
    ).astype(jnp.float32)
    grad_resid, grad_gain_one, grad_shift_one = norm1_pull(grad_normed)
    grad_attended = grad_resid.astype(jnp.bfloat16)
    grad_out_bias = jnp.sum(grad_attended.astype(jnp.float32), axis=0)
    grad_attn_rows = lax.all_gather(grad_attended, "mp", axis=0, tiled=True)
    grad_out = jnp.einsum("te,td->ed", context, grad_attn_rows, preferred_element_type=jnp.float32)
    grad_context = jnp.einsum(
        "td,ed->te", grad_attn_rows, w_out, preferred_element_type=jnp.float32
    )
    grad_context = grad_context.astype(jnp.bfloat16).reshape(rows_here, SEQ, heads_here, HD)

    def backward_row(row_items):
        return attend_back(
            row_items[0], row_items[1], row_items[2], row_items[3], row_items[4], row_items[5]
        )

    grad_queries, grad_keys, grad_values = lax.map(
        backward_row, (qkv[0], qkv[1], qkv[2], row_masks, log_total, grad_context)
    )
    grad_act = jnp.stack([grad_queries, grad_keys, grad_values]).reshape(
        3, rows_here * SEQ, local_width
    )
    grad_qkv = jnp.einsum("td,cte->cde", gathered, grad_act, preferred_element_type=jnp.float32)
    grad_qv_bias = jnp.sum(grad_act[::2].astype(jnp.float32), axis=1)
    grad_input = (
        grad_resid
        + lax.psum_scatter(
            jnp.einsum("cte,cde->td", grad_act, w_qkv, preferred_element_type=jnp.float32).astype(
                jnp.bfloat16
            ),
            "mp",
            scatter_dimension=0,
            tiled=True,
        ).astype(jnp.float32)
    ).astype(jnp.bfloat16)
    small_grads = lax.psum(
        (
            grad_out_bias,
            grad_gain_one,
            grad_shift_one,
            grad_down_bias,
            grad_gain_two,
            grad_shift_two,
        ),
        ("dp", "mp"),
    )
    grad_qkv, grad_qv_bias, grad_out, grad_up, grad_up_bias, grad_down = lax.psum(
        (grad_qkv, grad_qv_bias, grad_out, grad_up, grad_up_bias, grad_down), "dp"
    )
    return (
        tokens_out,
        pooled,
        grad_input,
        grad_qkv,
        grad_qv_bias,
        grad_out,
        small_grads[0],
        small_grads[1],
        small_grads[2],
        grad_up,
        grad_up_bias,
        grad_down,
        small_grads[3],
        small_grads[4],
        small_grads[5],
    )


def solution(mesh):
    in_specs = (
        P(("dp", "mp"), None),
        P("dp", None),
        P("dp"),
        P(None, None, "mp"),
        P(None, "mp"),
        P("mp", None),
        P(),
        P(),
        P(),
        P(None, "mp"),
        P("mp"),
        P("mp", None),
        P(),
        P(),
        P(),
        P(("dp", "mp"), None),
    )
    out_specs = (
        P(("dp", "mp"), None),
        P(("dp", "mp"), None),
        P(("dp", "mp"), None),
        P(None, None, "mp"),
        P(None, "mp"),
        P("mp", None),
        P(),
        P(),
        P(),
        P(None, "mp"),
        P("mp"),
        P("mp", None),
        P(),
        P(),
        P(),
    )
    return jax.shard_map(shards, mesh=mesh, in_specs=in_specs, out_specs=out_specs, check_vma=False)
```

profile of v0, /device:TPU:0, one launch (start us, length us, event | category | flops | bytes accessed | tf_op | source)
XLA Modules:
  0.0 1033.2 jit_solution(4419873463552302680)
XLA Ops:
  11.7 45.5 %all-gather.5.cloned.1.call-done = bf16[2048,768]{1,0:T(8,128)(2,1)} async-done(((bf16[1024,768]{1,0:T(8,128)(2,1)}), bf16[2048,768]{1,0:T(8,128)(2,1)}) %all-gather.5.cloned.1.call-update) | async-done | bytes 3145744 | tf_op jit(solution)/shard_map/all_gather | solution.py:95
  57.2 6.7 fusion.113
  87.9 29.8 %while.26 = (s32[]{:T(128)}, bf16[4,512,6,64]{1,3,2,0:T(8,128)(2,1)}, f32[4,6,512]{2,1,0:T(8,128)S(1)}, bf16[4,512,6,64]{1,3,2,0:T(8,128)(2,1)}, pred[4,512,512]...) while((s32[]{:T(128)}, ...), condition=%wide.region_5.6_spmd, body=%wide.region_2.5_spmd.sunk | while | flops 421721088 | bytes 21870692 | solution.py:110
  127.2 76.5 %reduce-scatter.5.cloned.1.call-done = f32[1024,768]{1,0:T(8,128)} async-done(((f32[2048,768]{1,0:T(8,128)}), f32[1024,768]{1,0:T(8,128)}) %reduce-scatter.5.cloned.1.call-update) | async-done | bytes 3145744 | tf_op jit(solution)/shard_map/reduce_scatter | solution.py:112
  210.0 45.0 %all-gather.7.cloned.1.call-done = bf16[2048,768]{1,0:T(8,128)(2,1)} async-done(((bf16[1024,768]{1,0:T(8,128)(2,1)}), bf16[2048,768]{1,0:T(8,128)(2,1)}) %all-gather.7.cloned.1.call-update) | async-done | bytes 3145744 | tf_op jit(solution)/shard_map/all_gather | solution.py:120
  255.0 12.6 %multiply_convert_fusion.1 = (bf16[2048,1536]{1,0:T(8,128)(2,1)S(1)}, f32[2048,1536]{1,0:T(8,128)}) fusion(f32[1536]{0:T(1024)S(1)} %convert_element_type.151, bf16[2048,768]{1,0:T(8,128)(2,1)} %all-gather.7.cloned.1.call-done, bf16[768,1536]{1,0:T(8,128)(2,1)S(1)} %copy-done), kind=kOutput, calls=%fused_computation.91 | convolution fusion | flops 4863295488 | bytes 24385536 | tf_op jit(solution)/shard_map/dot_general | solution.py:121
  270.2 6.3 convolution_convert_fusion.1
  277.3 42.8 %reduce-scatter.7.cloned.1.call-done = bf16[1024,768]{1,0:T(8,128)(2,1)} async-done(((bf16[2048,768]{1,0:T(8,128)(2,1)}), bf16[1024,768]{1,0:T(8,128)(2,1)}) %reduce-scatter.7.cloned.1.call-update) | async-done | bytes 1572880 | tf_op jit(solution)/shard_map/reduce_scatter | solution.py:127
  333.1 45.0 %all-gather.9.cloned.1.call-done = bf16[2048,768]{1,0:T(8,128)(2,1)} async-done(((bf16[1024,768]{1,0:T(8,128)(2,1)}), bf16[2048,768]{1,0:T(8,128)(2,1)}) %all-gather.9.cloned.1.call-update) | async-done | bytes 3145744 | tf_op jit(solution)/shard_map/all_gather | solution.py:150
  378.2 18.8 %convert_reduce_fusion = (f32[1536]{0:T(1024)S(1)}, bf16[2048,1536]{1,0:T(8,128)(2,1)S(1)}) fusion(bf16[2048,768]{1,0:T(8,128)(2,1)} %all-gather.9.cloned.1.call-done, bf16[1536,768]{1,0:T(8,128)(2,1)} %param.31, f32[2048,1536]{1,0:T(8,128)} %get-tuple-element.284, f32[1536]{0:T(1024)S(1)} %convert_element_type.151), kind=kOutput, calls=%fused_computation.90 | convolution fusion | flops 4916771328 | bytes 24391680 | tf_op jit(solution)/shard_map/td,fd->tf/dot_general | solution.py:154
  399.6 6.4 convolution_convert_fusion
  406.1 43.5 %reduce-scatter.9.cloned.1.call-done = bf16[1024,768]{1,0:T(8,128)(2,1)} async-done(((bf16[2048,768]{1,0:T(8,128)(2,1)}), bf16[1024,768]{1,0:T(8,128)(2,1)}) %reduce-scatter.9.cloned.1.call-update) | async-done | bytes 1572880 | tf_op jit(solution)/shard_map/reduce_scatter | solution.py:161
  460.8 45.0 %all-gather.11.cloned.1.call-done = bf16[2048,768]{1,0:T(8,128)(2,1)} async-done(((bf16[1024,768]{1,0:T(8,128)(2,1)}), bf16[2048,768]{1,0:T(8,128)(2,1)}) %all-gather.11.cloned.1.call-update) | async-done | bytes 3145744 | tf_op jit(solution)/shard_map/all_gather | solution.py:172
  505.8 4.8 convolution_convert_fusion.2
  521.6 145.1 %while.27 = (s32[]{:T(128)}, bf16[4,512,6,64]{1,3,2,0:T(8,128)(2,1)}, bf16[4,512,6,64]{1,3,2,0:T(8,128)(2,1)}, bf16[4,512,6,64]{1,3,2,0:T(8,128)(2,1)}, bf16[4,5...) while((s32[]{:T(128)}, ...), condition=%wide.region_20.21_spmd, body=%wide.region_18.20_spmd.sunk | while | flops 1048124416 | bytes 106542256 | solution.py:184
  531.7 13.3 %fusion.194 = bf16[4,512,6,64]{1,3,2,0:T(8,128)(2,1)} fusion(bf16[4,512,6,64]{1,3,2,0:T(8,128)(2,1)} %get-tuple-element.434, s32[]{:T(128)S(6)} %copy.117, f32[6,512,512]{1,2,0:T(8,128)} %fusion.191, f32[6,512,512]{1,2,0:T(8,128)} %copy-done.2, f32[6,512]{1,0:T(8,128)S(1)} %dynamic-slice_bitcast_fusion.7, ...), kind=kOutput, calls=%fused_computation.44.clone.1 | convolution fusion | flops 218828288 | bytes 26510336 | tf_op jit(solution)/shard_map/while/body/eval_jaxpr/hqk,qhd->khd/dot_general | solution.py:57
  545.1 13.1 %fusion.193 = bf16[4,512,6,64]{1,3,2,0:T(8,128)(2,1)} fusion(bf16[4,512,6,64]{1,3,2,0:T(8,128)(2,1)} %get-tuple-element.433, s32[]{:T(128)S(6)} %copy.117, f32[6,512,512]{1,2,0:T(8,128)} %fusion.191, f32[6,512,512]{1,2,0:T(8,128)} %copy-done.2, f32[6,512]{1,0:T(8,128)S(1)} %dynamic-slice_bitcast_fusion.7, ...), kind=kOutput, calls=%fused_computation.46.clone.1 | convolution fusion | flops 218828288 | bytes 26510336 | tf_op jit(solution)/shard_map/while/body/eval_jaxpr/hqk,khd->qhd/dot_general | solution.py:54
  567.9 13.3 %fusion.194 = bf16[4,512,6,64]{1,3,2,0:T(8,128)(2,1)} fusion(bf16[4,512,6,64]{1,3,2,0:T(8,128)(2,1)} %get-tuple-element.434, s32[]{:T(128)S(6)} %copy.117, f32[6,512,512]{1,2,0:T(8,128)} %fusion.191, f32[6,512,512]{1,2,0:T(8,128)} %copy-done.2, f32[6,512]{1,0:T(8,128)S(1)} %dynamic-slice_bitcast_fusion.7, ...), kind=kOutput, calls=%fused_computation.44.clone.1 | convolution fusion | flops 218828288 | bytes 26510336 | tf_op jit(solution)/shard_map/while/body/eval_jaxpr/hqk,qhd->khd/dot_general | solution.py:57
  581.2 13.1 %fusion.193 = bf16[4,512,6,64]{1,3,2,0:T(8,128)(2,1)} fusion(bf16[4,512,6,64]{1,3,2,0:T(8,128)(2,1)} %get-tuple-element.433, s32[]{:T(128)S(6)} %copy.117, f32[6,512,512]{1,2,0:T(8,128)} %fusion.191, f32[6,512,512]{1,2,0:T(8,128)} %copy-done.2, f32[6,512]{1,0:T(8,128)S(1)} %dynamic-slice_bitcast_fusion.7, ...), kind=kOutput, calls=%fused_computation.46.clone.1 | convolution fusion | flops 218828288 | bytes 26510336 | tf_op jit(solution)/shard_map/while/body/eval_jaxpr/hqk,khd->qhd/dot_general | solution.py:54
  604.0 13.3 %fusion.194 = bf16[4,512,6,64]{1,3,2,0:T(8,128)(2,1)} fusion(bf16[4,512,6,64]{1,3,2,0:T(8,128)(2,1)} %get-tuple-element.434, s32[]{:T(128)S(6)} %copy.117, f32[6,512,512]{1,2,0:T(8,128)} %fusion.191, f32[6,512,512]{1,2,0:T(8,128)} %copy-done.2, f32[6,512]{1,0:T(8,128)S(1)} %dynamic-slice_bitcast_fusion.7, ...), kind=kOutput, calls=%fused_computation.44.clone.1 | convolution fusion | flops 218828288 | bytes 26510336 | tf_op jit(solution)/shard_map/while/body/eval_jaxpr/hqk,qhd->khd/dot_general | solution.py:57
  617.3 13.1 %fusion.193 = bf16[4,512,6,64]{1,3,2,0:T(8,128)(2,1)} fusion(bf16[4,512,6,64]{1,3,2,0:T(8,128)(2,1)} %get-tuple-element.433, s32[]{:T(128)S(6)} %copy.117, f32[6,512,512]{1,2,0:T(8,128)} %fusion.191, f32[6,512,512]{1,2,0:T(8,128)} %copy-done.2, f32[6,512]{1,0:T(8,128)S(1)} %dynamic-slice_bitcast_fusion.7, ...), kind=kOutput, calls=%fused_computation.46.clone.1 | convolution fusion | flops 218828288 | bytes 26510336 | tf_op jit(solution)/shard_map/while/body/eval_jaxpr/hqk,khd->qhd/dot_general | solution.py:54
  640.1 13.3 %fusion.194 = bf16[4,512,6,64]{1,3,2,0:T(8,128)(2,1)} fusion(bf16[4,512,6,64]{1,3,2,0:T(8,128)(2,1)} %get-tuple-element.434, s32[]{:T(128)S(6)} %copy.117, f32[6,512,512]{1,2,0:T(8,128)} %fusion.191, f32[6,512,512]{1,2,0:T(8,128)} %copy-done.2, f32[6,512]{1,0:T(8,128)S(1)} %dynamic-slice_bitcast_fusion.7, ...), kind=kOutput, calls=%fused_computation.44.clone.1 | convolution fusion | flops 218828288 | bytes 26510336 | tf_op jit(solution)/shard_map/while/body/eval_jaxpr/hqk,qhd->khd/dot_general | solution.py:57
  653.4 13.1 %fusion.193 = bf16[4,512,6,64]{1,3,2,0:T(8,128)(2,1)} fusion(bf16[4,512,6,64]{1,3,2,0:T(8,128)(2,1)} %get-tuple-element.433, s32[]{:T(128)S(6)} %copy.117, f32[6,512,512]{1,2,0:T(8,128)} %fusion.191, f32[6,512,512]{1,2,0:T(8,128)} %copy-done.2, f32[6,512]{1,0:T(8,128)S(1)} %dynamic-slice_bitcast_fusion.7, ...), kind=kOutput, calls=%fused_computation.46.clone.1 | convolution fusion | flops 218828288 | bytes 26510336 | tf_op jit(solution)/shard_map/while/body/eval_jaxpr/hqk,khd->qhd/dot_general | solution.py:54
  694.5 8.5 bitcast_convert_fusion
  703.0 10.0 fusion.137
  713.0 9.7 fusion.136
  726.5 5.8 fusion.122
  736.9 41.1 %all-reduce = (f32[768]{0:T(1024)}, f32[768]{0:T(1024)}, f32[768]{0:T(1024)}, f32[768]{0:T(1024)}, f32[768]{0:T(1024)}, /*index=5*/f32[768]{0:T(1024)}) all-reduce(f32[768]{0:T(1024)S(1)} %get-tuple-element.262, f32[768]{0:T(1024)S(1)} %get-tuple-element.208, ...), channel_id=1, replica_groups=mesh['dp'=16,'mp'=2] {'dp','mp'}, use_global_device_ids=true, to_apply=%region_27.28 | all-reduce | flops 4608 | bytes 36864 | tf_op jit(solution)/shard_map/psum | solution.py:203
  780.7 64.3 %all-reduce.1 = (f32[2,384]{1,0:T(2,128)}, f32[1536]{0:T(1024)}) all-reduce(f32[2,384]{1,0:T(2,128)S(1)} %convert_reduce_fusion.1, f32[1536]{0:T(1024)S(1)} %get-tuple-element.285), channel_id=1, replica_groups=mesh['dp'=16,'mp'=2] {'dp'}, use_global_device_ids=true, to_apply=%region_24.25 | all-reduce | flops 2304 | bytes 18432 | tf_op jit(solution)/shard_map/psum | solution.py:214
  849.0 163.5 %all-reduce.5.cloned.1.call-done = (f32[3,768,384]{1,2,0:T(8,128)}, f32[384,768]{1,0:T(8,128)}, f32[768,1536]{1,0:T(8,128)}, f32[1536,768]{1,0:T(8,128)}) async-done(((f32[3,768,384]{1,2,0:T(8,128)}, f32[384,768]{1,0:T(8,128)}, f32[768,1536]{1,0:T(8,128)}, f32[1536,768]{1,0:T(8,128)}), (f32[3,768,384]{1,2,0:T(8,128)}, f32[384,768]{1,0:T(8,128)}, f32[768,1536]{1,0:T(8,128)}, ...) | async-done | bytes 14155792 | tf_op jit(solution)/shard_map/psum | solution.py:214
  1012.5 5.2 copy.91
  1018.7 5.5 copy.130
  (236 shorter events, 199.2 us)
Async XLA Ops:
  7.2 247.8 %copy-start = (bf16[768,1536]{1,0:T(8,128)(2,1)S(1)}, bf16[768,1536]{1,0:T(8,128)(2,1)}, u32[]{:S(2)}) copy-start(bf16[768,1536]{1,0:T(8,128)(2,1)} %param.29) | copy-start | bytes 7077892
  7.2 50.0 %all-gather.5.cloned.1.call-start = ((), (), s32[]{:S(2)}) async-start(), calls=%async_computation.4 | async-start | bytes 4718592 | tf_op jit(solution)/shard_map/all_gather | solution.py:95
  7.9 195.8 %reduce-scatter.5.cloned.1.call-start = ((), (), s32[]{:S(2)}) async-start(), calls=%async_computation.5 | async-start | bytes 9437184 | tf_op jit(solution)/shard_map/reduce_scatter | solution.py:112
  117.7 4.3 copy-start.19
  126.5 128.5 %all-gather.7.cloned.1.call-start = ((), (), s32[]{:S(2)}) async-start(), calls=%async_computation.6 | async-start | bytes 4718592 | tf_op jit(solution)/shard_map/all_gather | solution.py:120
  209.9 110.2 %reduce-scatter.7.cloned.1.call-start = ((), (), s32[]{:S(2)}) async-start(), calls=%async_computation.7 | async-start | bytes 4718592 | tf_op jit(solution)/shard_map/reduce_scatter | solution.py:127
  255.0 15.2 %copy-start.41 = (bf16[1536,768]{1,0:T(8,128)(2,1)S(1)}, bf16[1536,768]{1,0:T(8,128)(2,1)}, u32[]{:S(2)}) copy-start(bf16[1536,768]{1,0:T(8,128)(2,1)} %param.31) | copy-start | bytes 7077892
  276.6 101.5 %all-gather.9.cloned.1.call-start = ((), (), s32[]{:S(2)}) async-start(), calls=%async_computation.8 | async-start | bytes 4718592 | tf_op jit(solution)/shard_map/all_gather | solution.py:150
  277.3 50.6 %copy-start.23 = (f32[768]{0:T(1024)}, f32[768]{0:T(1024)S(1)}, u32[]{:S(2)}) copy-start(f32[768]{0:T(1024)S(1)} %convert_element_type.156) | copy-start | bytes 9220
  323.6 4.3 copy-start.4
  323.6 4.2 copy-start.21
  326.2 3.2 copy-start.25
  333.1 116.5 %reduce-scatter.9.cloned.1.call-start = ((), (), s32[]{:S(2)}) async-start(), calls=%async_computation.9 | async-start | bytes 4718592 | tf_op jit(solution)/shard_map/reduce_scatter | solution.py:161
  406.1 99.7 %all-gather.11.cloned.1.call-start = ((), (), s32[]{:S(2)}) async-start(), calls=%async_computation.10 | async-start | bytes 4718592 | tf_op jit(solution)/shard_map/all_gather | solution.py:172
  449.6 4.3 copy-start.17
  459.2 46.6 %copy-start.20 = (bf16[384,768]{1,0:T(8,128)(2,1)S(1)}, bf16[384,768]{1,0:T(8,128)(2,1)}, u32[]{:S(2)}) copy-start(bf16[384,768]{1,0:T(8,128)(2,1)} %param.25) | copy-start | bytes 1769476
  460.7 384.3 %reduce-scatter.11.cloned.1.call-start = ((), (), s32[]{:S(2)}) async-start(), calls=%async_computation.11 | async-start | bytes 4718592 | tf_op jit(solution)/shard_map/reduce_scatter | solution.py:194
  517.6 3.9 copy-start.7
  673.6 20.9 %copy-start.12 = (bf16[1,2048,384]{2,1,0:T(8,128)(2,1)}, bf16[1,2048,384]{2,1,0:T(8,128)(2,1)S(1)}, u32[]{:S(2)}) copy-start(bf16[1,2048,384]{2,1,0:T(8,128)(2,1)S(1)} %copy.89) | copy-start | bytes 4718596
  703.0 309.5 %all-reduce.5.cloned.1.call-start = ((), (), s32[]{:S(2)}) async-start(), calls=%async_computation.12 | async-start | bytes 28311552 | tf_op jit(solution)/shard_map/psum | solution.py:214
  703.0 10.0 copy-start.39
  713.0 9.7 copy-start.9
  713.0 9.7 copy-start.40
  722.7 3.7 copy-start.38
  732.3 4.7 copy-start.27
  732.3 4.7 copy-start.28
  732.3 4.6 copy-start.29
  732.3 45.7 %copy-start.14 = (bf16[1,2048,384]{2,1,0:T(8,128)(2,1)S(1)}, bf16[1,2048,384]{2,1,0:T(8,128)(2,1)}, u32[]{:S(2)}) copy-start(bf16[1,2048,384]{2,1,0:T(8,128)(2,1)} %copy-done.12) | copy-start | bytes 4718596
  1012.5 5.3 copy-start.18
  1017.7 6.5 slice-start
  1018.7 5.5 slice-start.1
  1018.7 7.7 copy-start.1
  (29 other events, 50.2 us)
Sparse Core Ops, SparseCore 0:
  9.6 47.6 all-gather.4
  126.6 77.0 reduce-scatter.4
  210.0 44.9 all-gather.6
  276.7 43.3 reduce-scatter.6
  333.2 44.9 all-gather.8
  406.2 43.3 reduce-scatter.8
  460.8 44.9 all-gather.10
  703.1 43.5 reduce-scatter.10
  752.4 260.0 all-reduce.4
where the time goes:
time: 1040 us; the launch traced here: 1030 us
  waiting for transfers between devices  508 us (49%)
  matrix products  265 us (25%)
  blocking collectives  105 us (10%)
  local copies, waits for them, and re-layouts  95.9 us (9%)
  other arithmetic  43.2 us (4%)
  between operations  14.5 us (1%)
    psum x1, waiting for transfers between devices, shards(): lax.psum((grad_qkv, grad_qv_bias, grad_out, grad_up, grad_up_bias, grad_d...  163 us
    reduce_scatter x1, waiting for transfers between devices, shards(): lax.psum_scatter(jnp.dot(context, w_out, preferred_element_type=jnp.float...  76.5 us
    psum x1, blocking collectives, shards(): lax.psum((grad_qkv, grad_qv_bias, grad_out, grad_up, grad_up_bias, grad_d...  64.3 us
    dot_general x4, matrix products, attend_back(): jnp.einsum('hqk,qhd->khd', grad_scores, queries, preferred_element_type=j...  53.3 us
    dot_general x4, matrix products, attend_back(): jnp.einsum('hqk,khd->qhd', grad_scores, key_rows, preferred_element_type=...  52.5 us
    all_gather x1, waiting for transfers between devices, shards(): gathered = lax.all_gather(tokens_in, 'mp', axis=0, tiled=True)  45.5 us
    all_gather x1, waiting for transfers between devices, shards(): grad_attn_rows = lax.all_gather(grad_attended, 'mp', axis=0, tiled=True)  45 us
    all_gather x1, waiting for transfers between devices, shards(): grad_branch_rows = lax.all_gather(grad_branch, 'mp', axis=0, tiled=True)  45 us
  transfers between devices with their start and end apart: 9, of which 8 were waited for; matrix products, arithmetic and copies ran while one was open for 4% of the time, Pallas kernels for 0%

commit v1 on v0

v1 whole, which is shorter than its diff:
```python
import functools

import jax
import jax.numpy as jnp
from jax import lax
from jax.experimental import pallas as pl
from jax.experimental.pallas import tpu as pltpu
from jax.sharding import PartitionSpec as P

HD = 64
SEQ = 512
PAIR = 128
EPSILON = 1e-12
SCORE_SCALE = 0.125
GELU_COEF = 0.7978845608028654
MASKED = -1e30
F32 = jnp.float32
BF16 = jnp.bfloat16

NT = (((1,), (1,)), ((), ()))
NN = (((1,), (0,)), ((), ()))
TN = (((0,), (0,)), ((), ()))


def dot(a, b, dims=NN):
    return lax.dot_general(a, b, dims, preferred_element_type=F32)


def attn_fwd_kernel(pad_ref, q_ref, k_ref, v_ref, qa_ref, ka_ref, ctx_ref, e_ref, rinv_ref):
    limit = SEQ - pad_ref[pl.program_id(0)]
    q, k = q_ref[0], k_ref[0]
    v_t = v_ref[0].astype(F32).T.astype(BF16)
    low = lax.broadcasted_iota(jnp.int32, (SEQ, PAIR), 1) < HD
    parts = []
    for h in range(2):
        own = low if h == 0 else ~low
        q_h = jnp.where(own, q, qa_ref[0])
        k_h = jnp.where(own, k, ka_ref[0])
        s = dot(k_h, q_h, NT)
        j = lax.broadcasted_iota(jnp.int32, (64, SEQ), 0) + (SEQ - 64)
        i = lax.broadcasted_iota(jnp.int32, (64, SEQ), 1)
        tail = jnp.where((j < limit) | (j == i), s[SEQ - 64 :], MASKED)
        s = jnp.concatenate([s[: SEQ - 64], tail], axis=0)
        peak = jnp.max(s, axis=0, keepdims=True)
        e = jnp.exp((s - peak) * SCORE_SCALE)
        rinv = 1.0 / jnp.sum(e, axis=0, keepdims=True)
        eb = e.astype(BF16)
        e_ref[h] = eb
        rinv_ref[0, 0, h : h + 1, :] = rinv
        parts.append(dot(v_t[h * HD : (h + 1) * HD], eb) * rinv)
    ctx_ref[...] = jnp.concatenate(parts, axis=0).T.astype(BF16)


def attn_fwd(qkv, pads, q_aug, k_aug):
    rows, pairs = pads.shape[0], qkv.shape[2] // PAIR
    width = qkv.shape[2]
    take = lambda c: pl.BlockSpec((1, SEQ, PAIR), lambda r, p, *_: (c, r, p))
    aug = pl.BlockSpec((1, SEQ, PAIR), lambda r, p, *_: (r, 0, 0))
    return pl.pallas_call(
        attn_fwd_kernel,
        grid_spec=pltpu.PrefetchScalarGridSpec(
            num_scalar_prefetch=1,
            grid=(rows, pairs),
            in_specs=[take(0), take(1), take(2), aug, aug],
            out_specs=[
                pl.BlockSpec((SEQ, PAIR), lambda r, p, *_: (r, p)),
                pl.BlockSpec((2, SEQ, SEQ), lambda r, p, *_: (r * pairs + p, 0, 0)),
                pl.BlockSpec((1, 1, 2, SEQ), lambda r, p, *_: (r, p, 0, 0)),
            ],
        ),
        out_shape=[
            jax.ShapeDtypeStruct((rows * SEQ, width), BF16),
            jax.ShapeDtypeStruct((rows * pairs * 2, SEQ, SEQ), BF16),
            jax.ShapeDtypeStruct((rows, pairs, 2, SEQ), F32),
        ],
        cost_estimate=pl.CostEstimate(
            flops=rows * pairs * 2 * 4 * SEQ * SEQ * PAIR * 2,
            bytes_accessed=rows * pairs * 2 * SEQ * SEQ * 2,
            transcendentals=rows * pairs * 2 * SEQ * SEQ,
        ),
        name="attn_fwd",
    )(pads, qkv, qkv, qkv, q_aug, k_aug)


def attn_bwd_kernel(q_ref, k_ref, v_ref, ctx_ref, dctx_ref, e_ref, rinv_ref, out_ref):
    q, k = q_ref[0], k_ref[0]
    v = v_ref[0]
    k_t = k.astype(F32).T.astype(BF16)
    d_t = dctx_ref[...].astype(F32).T
    c_t = ctx_ref[...].astype(F32).T
    lane = lax.broadcasted_iota(jnp.int32, (SEQ, PAIR), 1)
    row8 = lax.broadcasted_iota(jnp.int32, (8, SEQ), 0)
    low = lane < HD
    ones = jnp.where((lane & (HD - 1)) < 2, 1.0, 0.0).astype(BF16)
    dv, dk, dq = [], [], []
    for h in range(2):
        own = low if h == 0 else ~low
        rinv = rinv_ref[0, 0, h : h + 1, :]
        mine = d_t[h * HD : (h + 1) * HD] * rinv
        minus = -jnp.sum(mine * c_t[h * HD : (h + 1) * HD], axis=0, keepdims=True)
        high = minus.astype(BF16).astype(F32)
        extra = jnp.where(row8 == 0, high, jnp.where(row8 == 1, minus - high, 0.0))
        blank = jnp.zeros((HD - 8, SEQ), F32)
        stack = [mine, extra, blank] if h == 0 else [extra, blank, mine]
        g_t = jnp.concatenate(stack, axis=0).astype(BF16)
        v_h = jnp.where(own, v, ones)
        e = e_ref[h]
        d = e * dot(v_h, g_t).astype(BF16)
        dv.append(dot(e, g_t, NT))
        dk.append(dot(d, q))
        dq.append(dot(k_t[h * HD : (h + 1) * HD], d))
    out_ref[0] = (jnp.concatenate(dq, axis=0).T * SCORE_SCALE).astype(BF16)
    out_ref[1] = (jnp.where(low, dk[0], dk[1]) * SCORE_SCALE).astype(BF16)
    out_ref[2] = jnp.where(low, dv[0], dv[1]).astype(BF16)


def attn_bwd(qkv, ctx, dctx, e, rinv):
    rows, pairs = rinv.shape[0], rinv.shape[1]
    width = qkv.shape[2]
    take = lambda c: pl.BlockSpec((1, SEQ, PAIR), lambda r, p: (c, r, p))
    flat = pl.BlockSpec((SEQ, PAIR), lambda r, p: (r, p))
    return pl.pallas_call(
        attn_bwd_kernel,
        grid=(rows, pairs),
        in_specs=[
            take(0),
            take(1),
            take(2),
            flat,
            flat,
            pl.BlockSpec((2, SEQ, SEQ), lambda r, p: (r * pairs + p, 0, 0)),
            pl.BlockSpec((1, 1, 2, SEQ), lambda r, p: (r, p, 0, 0)),
        ],
        out_specs=pl.BlockSpec((3, SEQ, PAIR), lambda r, p: (0, r, p)),
        out_shape=jax.ShapeDtypeStruct((3, rows * SEQ, width), BF16),
        cost_estimate=pl.CostEstimate(
            flops=rows * pairs * 2 * 8 * SEQ * SEQ * PAIR * 2,
            bytes_accessed=rows * pairs * 2 * SEQ * SEQ * 2,
            transcendentals=0,
        ),
        name="attn_bwd",
    )(qkv, qkv, qkv, ctx, dctx, e, rinv)


def mask_lanes(seg_rows):
    ends = [seg_rows[:, 0]]
    for s in range(1, seg_rows.shape[1]):
        ends.append(ends[-1] + seg_rows[:, s])
    slot = jnp.arange(SEQ, dtype=jnp.int32)[None, :]
    segment = sum((slot >= end[:, None]).astype(jnp.int32) for end in ends)[..., None]
    lane = jnp.arange(PAIR, dtype=jnp.int32)[None, None, :] & (HD - 1)
    used = lane < seg_rows.shape[1]
    k_aug = jnp.where(used & (lane == segment), 1.0, 0.0).astype(BF16)
    q_aug = jnp.where(used & (lane != segment), MASKED, 0.0).astype(BF16)
    return q_aug, k_aug


def over_mp(x):
    n = lax.axis_size("mp")
    return lax.ppermute(x, "mp", [(i, i ^ 1) for i in range(n)])


def over_dp(x, bit):
    n = lax.axis_size("dp")
    return lax.ppermute(x, "dp", [(i, i ^ bit) for i in range(n)])


def place_kernel(n, rows, at_ref, *refs):
    out_ref = refs[-1]
    k = 0
    for ref in refs[:-1]:
        for i in range(ref.shape[-2] // rows):
            spot = pl.ds(pl.multiple_of(at_ref[k], 16), rows)
            take = pl.ds(i * rows, rows)
            if len(out_ref.shape) == 2:
                out_ref[spot, :] = ref[take, :].astype(out_ref.dtype)
            else:
                out_ref[:, spot, :] = ref[:, take, :].astype(out_ref.dtype)
            k += 1


def place(pieces, at, rows, dtype):
    total = sum(piece.shape[-2] for piece in pieces)
    n = total // rows
    lead, cols = pieces[0].shape[:-2], pieces[0].shape[-1]
    size = total * cols * (lead[0] if lead else 1)
    whole = pl.BlockSpec(memory_space=pltpu.VMEM)
    return pl.pallas_call(
        functools.partial(place_kernel, n, rows),
        in_specs=[pl.BlockSpec(memory_space=pltpu.SMEM)] + [whole] * len(pieces),
        out_specs=whole,
        out_shape=jax.ShapeDtypeStruct(lead + (total, cols), dtype),
        compiler_params=pltpu.CompilerParams(vmem_limit_bytes=32 * 2**20),
        cost_estimate=pl.CostEstimate(flops=0, bytes_accessed=6 * size, transcendentals=0),
        name="place",
    )(at, *pieces)


def fetch_other(w, quarter):
    rows = w.shape[-2] // 4
    own = lax.dynamic_slice_in_dim(w, quarter * rows, rows, w.ndim - 2)
    first = over_mp(own)
    second = over_dp(first, 2)
    third, fourth = over_dp(first, 1), over_dp(second, 1)
    at = jnp.stack([quarter, quarter ^ 2, quarter ^ 1, quarter ^ 3]).astype(jnp.int32) * rows
    return place([first, second, third, fourth], at, rows, w.dtype)


SPLIT_BITS = (1, 2, 4, 8)


def reduce_all(mine, other, me):
    rows = mine.shape[0]

    def halves(x, bit):
        half = x.shape[0] // 2
        up = (me & bit) // bit
        keep = lax.dynamic_slice_in_dim(x, up * half, half, 0)
        send = lax.dynamic_slice_in_dim(x, (1 - up) * half, half, 0)
        return keep, send

    add = lambda a, b: (a.astype(F32) + b.astype(F32)).astype(BF16)
    keep_o, send_o = halves(other, 1)
    keep_m, send_m = halves(mine, 1)
    other = add(keep_o, over_dp(send_o, 1))
    mine = add(keep_m, over_dp(send_m, 1))
    mine = add(mine, over_mp(other))
    for bit in SPLIT_BITS[1:]:
        keep, send = halves(mine, bit)
        mine = add(keep, over_dp(send, bit))
    bit = 2 * SPLIT_BITS[-1]
    while bit < lax.axis_size("dp"):
        mine = add(mine, over_dp(mine, bit))
        bit *= 2
    held, order = [mine], [0]
    for bit in reversed(SPLIT_BITS):
        full = jnp.concatenate(held, axis=0) if len(held) > 1 else held[0]
        held.append(over_dp(full, bit))
        order += [o ^ bit for o in order]
    size = len(SPLIT_BITS)
    at = []
    for o in order:
        who = me ^ o
        spot = sum(((who >> b) & 1) << (size - 1 - b) for b in range(size))
        at.append(spot * (rows // 16))
    return place(held, jnp.stack(at).astype(jnp.int32), rows // 16, F32)


def layer_norm(v):
    centered = v - jnp.mean(v, axis=-1, keepdims=True)
    rstd = lax.rsqrt(jnp.mean(centered * centered, axis=-1, keepdims=True) + EPSILON)
    return centered * rstd, rstd


def layer_norm_back(dy, xhat, rstd, gain):
    dg = dy * gain
    return rstd * (
        dg
        - jnp.mean(dg, axis=-1, keepdims=True)
        - xhat * jnp.mean(dg * xhat, axis=-1, keepdims=True)
    )


def gelu_and_slope(u):
    inner = GELU_COEF * (u + 0.044715 * u * u * u)
    t = jnp.tanh(inner)
    act = 0.5 * u * (1.0 + t)
    slope = 0.5 * (1.0 + t) + 0.5 * u * (1.0 - t * t) * GELU_COEF * (1.0 + 3 * 0.044715 * u * u)
    return act, slope


def shards(
    tokens_in,
    seg_lengths,
    pad_counts,
    w_qkv,
    qv_bias,
    w_out,
    out_bias,
    norm1_gain,
    norm1_bias,
    w_up,
    up_bias,
    w_down,
    down_bias,
    norm2_gain,
    norm2_bias,
    cotangent,
):
    tokens, width = tokens_in.shape
    rows_here = tokens // SEQ
    local = w_qkv.shape[2]
    units = w_up.shape[1]
    me = lax.axis_index("dp")
    quarter = me & 3
    start = lax.axis_index("mp") * rows_here
    seg_rows = lax.dynamic_slice_in_dim(seg_lengths, start, rows_here, 0)
    pads = lax.dynamic_slice_in_dim(pad_counts, start, rows_here, 0)

    small_w = jnp.concatenate([qv_bias.reshape(-1), up_bias])
    small_o = over_mp(small_w)
    qv_biases = (qv_bias, small_o[: 2 * local].reshape(2, local))
    up_biases = (up_bias, small_o[2 * local :])
    w_qkvs = (w_qkv, fetch_other(w_qkv, quarter))
    w_outs = (w_out, fetch_other(w_out, quarter))
    w_ups = (w_up, fetch_other(w_up, quarter))
    w_downs = (w_down, fetch_other(w_down, quarter))

    q_aug, k_aug = mask_lanes(seg_rows)
    qkv, ctx, probs, rinv = [], [], [], []
    for h in range(2):
        b = qv_biases[h].astype(F32)
        bias = jnp.stack([b[0], jnp.zeros_like(b[0]), b[1]])
        projected = jnp.einsum("td,cde->cte", tokens_in, w_qkvs[h], preferred_element_type=F32)
        qkv.append((projected + bias[:, None, :]).astype(BF16))
        c, e, r = attn_fwd(qkv[h], pads, q_aug, k_aug)
        ctx.append(c)
        probs.append(e)
        rinv.append(r)

    gain_one, shift_one = norm1_gain.astype(F32), norm1_bias.astype(F32)
    gain_two, shift_two = norm2_gain.astype(F32), norm2_bias.astype(F32)
    attended = dot(ctx[0], w_outs[0]) + dot(ctx[1], w_outs[1]) + out_bias.astype(F32)
    xhat_one, rstd_one = layer_norm(tokens_in.astype(F32) + attended)
    normed = xhat_one * gain_one + shift_one
    mid = normed.astype(BF16)
    act, slope = [], []
    for h in range(2):
        a, s = gelu_and_slope(dot(mid, w_ups[h]) + up_biases[h].astype(F32))
        act.append(a.astype(BF16))
        slope.append(s.astype(BF16))
    second = (
        normed + dot(act[0], w_downs[0]) + dot(act[1], w_downs[1]) + down_bias.astype(F32)
    )
    xhat_two, rstd_two = layer_norm(second)
    final_rows = xhat_two * gain_two + shift_two
    tokens_out = final_rows.astype(BF16)
    count = SEQ - pads
    usable = (jnp.arange(SEQ, dtype=jnp.int32)[None, :] < count[:, None]).astype(F32)
    pooled = (
        jnp.sum(final_rows.reshape(rows_here, SEQ, width) * usable[..., None], axis=1)
        / count.astype(F32)[:, None]
    )

    dy = cotangent.astype(F32)
    grad_gain_two, grad_shift_two = jnp.sum(dy * xhat_two, axis=0), jnp.sum(dy, axis=0)
    grad_second = layer_norm_back(dy, xhat_two, rstd_two, gain_two)
    grad_branch = grad_second.astype(BF16)
    grad_down_bias = jnp.sum(grad_branch.astype(F32), axis=0)
    grad_down = [dot(act[h], grad_branch, TN).astype(BF16) for h in range(2)]
    grad_down = reduce_all(*grad_down, me)
    upper = [
        (dot(grad_branch, w_downs[h], NT) * slope[h].astype(F32)).astype(BF16) for h in range(2)
    ]
    grad_up_bias = [jnp.sum(u.astype(F32), axis=0) for u in upper]
    grad_up = [dot(mid, upper[h], TN).astype(BF16) for h in range(2)]
    grad_up = reduce_all(*grad_up, me)
    grad_normed = grad_second + dot(upper[0], w_ups[0], NT) + dot(upper[1], w_ups[1], NT)
    grad_gain_one = jnp.sum(grad_normed * xhat_one, axis=0)
    grad_shift_one = jnp.sum(grad_normed, axis=0)
    grad_resid = layer_norm_back(grad_normed, xhat_one, rstd_one, gain_one)
    grad_attended = grad_resid.astype(BF16)
    grad_out_bias = jnp.sum(grad_attended.astype(F32), axis=0)

    total, grad_qv_bias, grad_attn = grad_resid, [], []
    for h in range(2):
        grad_ctx = dot(grad_attended, w_outs[h], NT).astype(BF16)
        grad_act = attn_bwd(qkv[h], ctx[h], grad_ctx, probs[h], rinv[h])
        grad_qv_bias.append(jnp.sum(grad_act[::2].astype(F32), axis=1))
        g = jnp.einsum("td,cte->cde", tokens_in, grad_act, preferred_element_type=F32)
        g = g.astype(BF16).reshape(3 * width, local)
        g_out = dot(grad_attended, ctx[h], TN).astype(BF16)
        grad_attn.append(jnp.concatenate([g, g_out], axis=0))
        total = total + jnp.einsum(
            "cte,cde->td", grad_act, w_qkvs[h], preferred_element_type=F32
        )
    grad_input = total.astype(BF16)
    grad_attn = reduce_all(*grad_attn, me)
    grad_qkv = grad_attn[: 3 * width].reshape(3, width, local)
    grad_out = grad_attn[3 * width :].T

    same = jnp.concatenate(
        [
            grad_out_bias,
            grad_gain_one,
            grad_shift_one,
            grad_down_bias,
            grad_gain_two,
            grad_shift_two,
        ]
    )
    own = [jnp.concatenate([grad_qv_bias[h].reshape(-1), grad_up_bias[h]]) for h in range(2)]
    small = jnp.concatenate([same, own[0]]) + over_mp(jnp.concatenate([same, own[1]]))
    bit = 1
    while bit < lax.axis_size("dp"):
        small = small + over_dp(small, bit)
        bit *= 2
    vectors = small[: 6 * width].reshape(6, width)
    grad_qv_bias = small[6 * width : 6 * width + 2 * local].reshape(2, local)
    grad_up_bias = small[6 * width + 2 * local :]
    return (
        tokens_out,
        pooled,
        grad_input,
        grad_qkv,
        grad_qv_bias,
        grad_out,
        vectors[0],
        vectors[1],
        vectors[2],
        grad_up,
        grad_up_bias,
        grad_down,
        vectors[3],
        vectors[4],
        vectors[5],
    )


def solution(mesh):
    token = P(("dp", "mp"), None)
    in_specs = (
        token,
        P("dp", None),
        P("dp"),
        P(None, None, "mp"),
        P(None, "mp"),
        P("mp", None),
        P(),
        P(),
        P(),
        P(None, "mp"),
        P("mp"),
        P("mp", None),
        P(),
        P(),
        P(),
        token,
    )
    out_specs = (
        token,
        token,
        token,
        P(None, None, "mp"),
        P(None, "mp"),
        P("mp", None),
        P(),
        P(),
        P(),
        P(None, "mp"),
        P("mp"),
        P("mp", None),
        P(),
        P(),
        P(),
    )
    return jax.shard_map(shards, mesh=mesh, in_specs=in_specs, out_specs=out_specs, check_vma=False)
```

time: 1040 us -> 440 us (0.42)
  waiting for transfers between devices: 508 us -> 150 us
  matrix products: 265 us -> 97.7 us
  blocking collectives: 105 us -> 0 us
  local copies, waits for them, and re-layouts: 95.9 us -> 31.3 us
  Pallas kernels: 0 us -> 59.3 us
  starting transfers between devices: 0.59 us -> 43.7 us
  between operations: 14.5 us -> 2.17 us
    all_gather x4 -> x0, waiting for transfers between devices: 181 us -> none  [the longest x1 45.5 us: shards(): gathered = lax.all_gather(tokens_in, 'mp', axis=0, tiled=True)]
    dot_general x40 -> x24, matrix products: 265 us -> 97.7 us  [the longest x18 71.7 us: dot(): return lax.dot_general(a, b, dims, preferred_element_type=F32)]
    psum x1 -> x0, waiting for transfers between devices: 163 us -> none  [shards(): lax.psum((grad_qkv, grad_qv_bias, grad_out, grad_up, grad_up_bias, grad_d...]
    reduce_scatter x4 -> x0, waiting for transfers between devices: 163 us -> none  [the longest x1 76.5 us: shards(): lax.psum_scatter(jnp.dot(context, w_out, preferred_element_type=jnp.float...]
    ppermute x0 -> x52, waiting for transfers between devices: none -> 150 us  [the longest x43 83.6 us: over_dp(): return lax.ppermute(x, 'dp', [(i, i ^ bit) for i in range(n)])]
    psum x2 -> x0, blocking collectives: 105 us -> none  [the longest x1 64.3 us: shards(): lax.psum((grad_qkv, grad_qv_bias, grad_out, grad_up, grad_up_bias, grad_d...]
    pallas_call x0 -> x11, Pallas kernels: none -> 59.3 us  [the longest x2 23.2 us: attn_fwd(): pl.pallas_call(attn_fwd_kernel, grid_spec=pltpu.PrefetchScalarGridSpec(nu...]
    ppermute x0 -> x52, starting transfers between devices: none -> 43.7 us  [the longest x43 32.7 us: over_dp(): return lax.ppermute(x, 'dp', [(i, i ^ bit) for i in range(n)])]
  transfers between devices with their start and end apart: 9 -> 52, of which waited for: 8 -> 17; matrix products, arithmetic and copies ran while one was open for 4% -> 23% of each run, Pallas kernels for 0% -> 7%
where the time goes in v1:
time: 440 us; the launch traced here: 435 us
  waiting for transfers between devices  150 us (34%)
  matrix products  97.7 us (22%)
  Pallas kernels  59.3 us (13%)
  other arithmetic  50.8 us (12%)
  starting transfers between devices  43.7 us (10%)
  local copies, waits for them, and re-layouts  31.3 us (7%)
    ppermute x43, waiting for transfers between devices, over_dp(): return lax.ppermute(x, 'dp', [(i, i ^ bit) for i in range(n)])  83.6 us
    dot_general x18, matrix products, dot(): return lax.dot_general(a, b, dims, preferred_element_type=F32)  71.7 us
    ppermute x9, waiting for transfers between devices, over_mp(): return lax.ppermute(x, 'mp', [(i, i ^ 1) for i in range(n)])  66.5 us
    ppermute x43, starting transfers between devices, over_dp(): return lax.ppermute(x, 'dp', [(i, i ^ bit) for i in range(n)])  32.7 us
    pallas_call x2, Pallas kernels, attn_fwd(): pl.pallas_call(attn_fwd_kernel, grid_spec=pltpu.PrefetchScalarGridSpec(nu...  23.2 us
    pallas_call x2, Pallas kernels, attn_bwd(): pl.pallas_call(attn_bwd_kernel, grid=(rows, pairs), in_specs=[take(0), ta...  21.6 us
    pallas_call x7, Pallas kernels, place(): pl.pallas_call(functools.partial(place_kernel, n, rows), in_specs=[pl.Blo...  14.5 us
    convert_element_type x15, other arithmetic, reduce_all(): add = lambda a, b: (a.astype(F32) + b.astype(F32)).astype(BF16)  11.5 us
  transfers between devices with their start and end apart: 52, of which 17 were waited for; matrix products, arithmetic and copies ran while one was open for 23% of the time, Pallas kernels for 7%

profile of v1, /device:TPU:0, one launch (start us, length us, event | category | flops | bytes accessed | tf_op | source)
XLA Modules:
  0.0 435.2 jit_solution(8890037458898467921)
XLA Ops:
  31.5 5.6 %fusion.21.q_ref.k_ref.v_ref = bf16[3,1024,384]{2,1,0:T(8,128)(2,1)} fusion(f32[3,384]{1,0:T(4,128)S(1)} %get-tuple-element.93, bf16[3,768,384]{2,1,0:T(8,128)(2,1)} %param.19, bf16[1024,768]{1,0:T(8,128)(2,1)} %param.16), kind=kOutput, calls=%fused_computation.68 | convolution fusion | flops 1814298624 | bytes 5706240 | tf_op jit(solution)/shard_map/td,cde->cte/dot_general | solution.py:314
  39.1 4.5 %collective-permute-done.13.refs_0_ = bf16[384,768]{1,0:T(8,128)(2,1)S(1)} collective-permute-done((bf16[384,768]{1,0:T(8,128)(2,1)}, bf16[384,768]{1,0:T(8,128)(2,1)S(1)}, u32[]{:S(2)}, u32[]{:S(2)}) %collective-permute-start.13) | collective-permute-done | bytes 589856 | tf_op jit(solution)/shard_map/ppermute | solution.py:160
  45.4 11.6 %attn_fwd.2 = (bf16[1024,384]{1,0:T(8,128)(2,1)}, bf16[12,512,512]{2,1,0:T(8,128)(2,1)}, f32[2,3,2,512]{3,2,1,0:T(2,128)}) custom-call(s32[2]{0:T(128)} %copy-done.64, bf16[3,1024,384]{2,1,0:T(8,128)(2,1)} %fusion.21.q_ref.k_ref.v_ref, bf16[3,1024,384]{2,1,0:T(8,128)(2,1)} %fusion.21.q_ref.k_ref.v_ref, bf16[3,1024,384]{2,1,0:T(8,128)(2,1)} %fusion.21.q_ref.k_ref.v_ref, ...), custom_call_target="tpu_custom_call" | custom-call | flops 3221225472 | bytes 6291456 | tf_op jit(solution)/shard_map/attn_fwd/pallas_call | solution.py:59
  57.8 3.9 fusion.44
  75.5 11.6 %attn_fwd.3 = (bf16[1024,384]{1,0:T(8,128)(2,1)}, bf16[12,512,512]{2,1,0:T(8,128)(2,1)}, f32[2,3,2,512]{3,2,1,0:T(2,128)}) custom-call(s32[2]{0:T(128)} %copy-done.64, bf16[3,1024,384]{2,1,0:T(8,128)(2,1)} %fusion.22.q_ref.k_ref.v_ref, bf16[3,1024,384]{2,1,0:T(8,128)(2,1)} %fusion.22.q_ref.k_ref.v_ref, bf16[3,1024,384]{2,1,0:T(8,128)(2,1)} %fusion.22.q_ref.k_ref.v_ref, ...), custom_call_target="tpu_custom_call" | custom-call | flops 3221225472 | bytes 6291456 | tf_op jit(solution)/shard_map/attn_fwd/pallas_call | solution.py:59
  92.2 5.5 %multiply_convert_fusion.3 = (bf16[1024,1536]{1,0:T(8,128)(2,1)S(1)}, f32[1024,1536]{1,0:T(8,128)}) fusion(f32[1536]{0:T(1024)S(1)} %copy-done.52, bf16[1024,768]{1,0:T(8,128)(2,1)S(1)} %fusion.20, bf16[768,1536]{1,0:T(8,128)(2,1)S(1)} %copy-done), kind=kOutput, calls=%fused_computation.21 | convolution fusion | flops 2431647744 | bytes 13375488 | tf_op jit(solution)/shard_map/dot_general | solution.py:26
  97.8 4.3 fusion.45
  108.1 6.2 %fusion.43 = (f32[1024]{0:T(1024)S(1)}, f32[1024,768]{1,0:T(8,128)S(1)}) fusion(f32[768]{0:T(1024)S(1)} %copy-done.59, bf16[1536,768]{1,0:T(8,128)(2,1)S(1)} %place.10, f32[1024,1536]{1,0:T(8,128)S(1)} %fusion.46, f32[1536]{0:T(1024)S(1)} %copy-done.53, f32[1024,768]{1,0:T(8,128)} %fusion.45, f32[768]{0:T(1024)S(1)} %copy-done.43, ...), kind=kOutput, calls=%fused_computation.189 | convolution fusion | flops 2437938176 | bytes 18115584 | tf_op jit(solution)/shard_map/dot_general | solution.py:26
  120.3 5.0 %convolution_convert_fusion = bf16[1536,768]{1,0:T(8,128)(2,1)} fusion(bf16[1024,768]{1,0:T(8,128)(2,1)S(1)} %get-tuple-element.55, f32[1024,1536]{1,0:T(8,128)S(1)} %fusion.46, f32[1536]{0:T(1024)S(1)} %copy-done.53), kind=kOutput, calls=%fused_computation.30 | convolution fusion | flops 2432827392 | bytes 10229760 | tf_op jit(solution)/shard_map/dot_general | solution.py:26
  125.3 4.0 convolution_convert_fusion.1
  129.3 7.4 %convert_reduce_fusion = (f32[1536]{0:T(1024)}, bf16[1024,1536]{1,0:T(8,128)(2,1)S(1)}) fusion(f32[1024,1536]{1,0:T(8,128)S(1)} %fusion.46, f32[1536]{0:T(1024)S(1)} %copy-done.53, bf16[1024,768]{1,0:T(8,128)(2,1)S(1)} %get-tuple-element.55, bf16[1536,768]{1,0:T(8,128)(2,1)S(1)} %place.10), kind=kOutput, calls=%fused_computation.16 | convolution fusion | flops 2453666304 | bytes 13381632 | tf_op jit(solution)/shard_map/dot_general | solution.py:26
  136.7 8.3 %convert_reduce_fusion.1 = (f32[1536]{0:T(1024)}, bf16[1024,1536]{1,0:T(8,128)(2,1)S(1)}) fusion(f32[1024,1536]{1,0:T(8,128)} %get-tuple-element.97, f32[1536]{0:T(1024)S(1)} %copy-done.52, bf16[1024,768]{1,0:T(8,128)(2,1)S(1)} %get-tuple-element.55, bf16[1536,768]{1,0:T(8,128)(2,1)S(1)} %copy-done.34), kind=kOutput, calls=%fused_computation.17 | convolution fusion | flops 2453666304 | bytes 13381632 | tf_op jit(solution)/shard_map/dot_general | solution.py:26
  145.0 4.1 convolution_convert_fusion.3
  154.7 4.5 %multiply_reduce_fusion = (f32[768]{0:T(1024)}, f32[1024]{0:T(1024)S(1)}, f32[1024]{0:T(1024)S(1)}, f32[768]{0:T(1024)}, f32[1024,768]{1,0:T(8,128)S(1)}) fusion(f32[1024,768]{1,0:T(8,128)S(1)} %get-tuple-element.95, f32[1024]{0:T(1024)S(1)} %add_rsqrt_fusion.1, f32[1024]{0:T(1024)S(1)} %broadcast_multiply_fusion.5, f32[768]{0:T(1024)S(1)} %copy-done.41, ...), kind=kOutput, calls=%fused_computation.44 | convolution fusion | flops 2430857728 | bytes 19705856 | tf_op jit(solution)/shard_map/dot_general | solution.py:26
  165.4 10.8 %attn_bwd.2 = bf16[3,1024,384]{2,1,0:T(8,128)(2,1)} custom-call(bf16[3,1024,384]{2,1,0:T(8,128)(2,1)} %fusion.21.q_ref.k_ref.v_ref, bf16[3,1024,384]{2,1,0:T(8,128)(2,1)} %fusion.21.q_ref.k_ref.v_ref, bf16[3,1024,384]{2,1,0:T(8,128)(2,1)} %fusion.21.q_ref.k_ref.v_ref, bf16[1024,384]{1,0:T(8,128)(2,1)} %get-tuple-element.21.ctx_ref, ...), custom_call_target="tpu_custom_call" | custom-call | flops 6442450944 | bytes 6291456 | tf_op jit(solution)/shard_map/attn_bwd/pallas_call | solution.py:122
  177.9 5.6 %convert_bitcast_fusion.1 = bf16[3,768,384]{1,2,0:T(8,128)(2,1)} fusion(bf16[3,1024,384]{2,1,0:T(8,128)(2,1)} %attn_bwd.2, bf16[1024,768]{1,0:T(8,128)(2,1)} %param.16), kind=kOutput, calls=%fused_computation.80 | convolution fusion | flops 1812824064 | bytes 5701632 | tf_op jit(solution)/shard_map/td,cte->cde/dot_general | solution.py:370
  185.3 10.7 %attn_bwd.3 = bf16[3,1024,384]{2,1,0:T(8,128)(2,1)} custom-call(bf16[3,1024,384]{2,1,0:T(8,128)(2,1)} %fusion.22.q_ref.k_ref.v_ref, bf16[3,1024,384]{2,1,0:T(8,128)(2,1)} %fusion.22.q_ref.k_ref.v_ref, bf16[3,1024,384]{2,1,0:T(8,128)(2,1)} %fusion.22.q_ref.k_ref.v_ref, bf16[1024,384]{1,0:T(8,128)(2,1)} %get-tuple-element.22.ctx_ref, ...), custom_call_target="tpu_custom_call" | custom-call | flops 6442450944 | bytes 6291456 | tf_op jit(solution)/shard_map/attn_bwd/pallas_call | solution.py:122
  197.8 5.5 %convert_bitcast_fusion = bf16[3,768,384]{1,2,0:T(8,128)(2,1)} fusion(bf16[3,1024,384]{2,1,0:T(8,128)(2,1)} %attn_bwd.3, bf16[1024,768]{1,0:T(8,128)(2,1)} %param.16), kind=kOutput, calls=%fused_computation.79 | convolution fusion | flops 1812824064 | bytes 5701632 | tf_op jit(solution)/shard_map/td,cte->cde/dot_general | solution.py:370
  230.8 20.1 %collective-permute-done.44 = bf16[768,768]{1,0:T(8,128)(2,1)S(1)} collective-permute-done((bf16[768,768]{1,0:T(8,128)(2,1)S(1)}, bf16[768,768]{1,0:T(8,128)(2,1)S(1)}, u32[]{:S(2)}, u32[]{:S(2)}) %collective-permute-start.44) | collective-permute-done | bytes 1179680 | tf_op jit(solution)/shard_map/ppermute | solution.py:160
  255.8 20.4 %collective-permute-done.34 = bf16[384,1536]{1,0:T(8,128)(2,1)S(1)} collective-permute-done((bf16[384,1536]{1,0:T(8,128)(2,1)S(1)}, bf16[384,1536]{1,0:T(8,128)(2,1)S(1)}, u32[]{:S(2)}, u32[]{:S(2)}) %collective-permute-start.34) | collective-permute-done | bytes 1179680 | tf_op jit(solution)/shard_map/ppermute | solution.py:160
  279.5 21.5 %collective-permute-done.19 = bf16[1536,384]{1,0:T(8,128)(2,1)S(1)} collective-permute-done((bf16[1536,384]{1,0:T(8,128)(2,1)S(1)}, bf16[1536,384]{1,0:T(8,128)(2,1)S(1)}, u32[]{:S(2)}, u32[]{:S(2)}) %collective-permute-start.19) | collective-permute-done | bytes 1179680 | tf_op jit(solution)/shard_map/ppermute | solution.py:160
  307.0 10.9 %collective-permute-done.20 = bf16[768,384]{1,0:T(8,128)(2,1)S(1)} collective-permute-done((bf16[768,384]{1,0:T(8,128)(2,1)S(1)}, bf16[768,384]{1,0:T(8,128)(2,1)S(1)}, u32[]{:S(2)}, u32[]{:S(2)}) %collective-permute-start.20) | collective-permute-done | bytes 589856 | tf_op jit(solution)/shard_map/ppermute | solution.py:165
  323.1 8.0 %collective-permute-done.21 = bf16[384,384]{1,0:T(8,128)(2,1)S(1)} collective-permute-done((bf16[384,384]{1,0:T(8,128)(2,1)S(1)}, bf16[384,384]{1,0:T(8,128)(2,1)S(1)}, u32[]{:S(2)}, u32[]{:S(2)}) %collective-permute-start.21) | collective-permute-done | bytes 294944 | tf_op jit(solution)/shard_map/ppermute | solution.py:165
  334.3 10.3 %collective-permute-done.37 = bf16[48,1536]{1,0:T(8,128)(2,1)S(1)} collective-permute-done((bf16[48,1536]{1,0:T(8,128)(2,1)S(1)}, bf16[48,1536]{1,0:T(8,128)(2,1)S(1)}, u32[]{:S(2)}, u32[]{:S(2)}) %collective-permute-start.37) | collective-permute-done | bytes 147488 | tf_op jit(solution)/shard_map/ppermute | solution.py:165
  348.1 7.5 %collective-permute-done.48.refs_1_ = bf16[96,768]{1,0:T(8,128)(2,1)S(1)} collective-permute-done((bf16[96,768]{1,0:T(8,128)(2,1)S(1)}, bf16[96,768]{1,0:T(8,128)(2,1)S(1)}, u32[]{:S(2)}, u32[]{:S(2)}) %collective-permute-start.48) | collective-permute-done | bytes 147488 | tf_op jit(solution)/shard_map/ppermute | solution.py:165
  368.8 4.7 %collective-permute-done.39.refs_2_ = bf16[96,1536]{1,0:T(8,128)(2,1)S(1)} collective-permute-done((bf16[96,1536]{1,0:T(8,128)(2,1)S(1)}, bf16[96,1536]{1,0:T(8,128)(2,1)S(1)}, u32[]{:S(2)}, u32[]{:S(2)}) %collective-permute-start.39) | collective-permute-done | bytes 294944 | tf_op jit(solution)/shard_map/ppermute | solution.py:165
  375.2 4.6 %collective-permute-done.24.refs_2_ = bf16[384,384]{1,0:T(8,128)(2,1)S(1)} collective-permute-done((bf16[384,384]{1,0:T(8,128)(2,1)S(1)}, bf16[384,384]{1,0:T(8,128)(2,1)S(1)}, u32[]{:S(2)}, u32[]{:S(2)}) %collective-permute-start.24) | collective-permute-done | bytes 294944 | tf_op jit(solution)/shard_map/ppermute | solution.py:165
  384.9 11.2 %collective-permute-done.40.refs_3_ = bf16[192,1536]{1,0:T(8,128)(2,1)S(1)} collective-permute-done((bf16[192,1536]{1,0:T(8,128)(2,1)S(1)}, bf16[192,1536]{1,0:T(8,128)(2,1)S(1)}, u32[]{:S(2)}, u32[]{:S(2)}) %collective-permute-start.40) | collective-permute-done | bytes 589856 | tf_op jit(solution)/shard_map/ppermute | solution.py:165
  397.4 10.4 %collective-permute-done.25.refs_3_ = bf16[768,384]{1,0:T(8,128)(2,1)S(1)} collective-permute-done((bf16[768,384]{1,0:T(8,128)(2,1)S(1)}, bf16[768,384]{1,0:T(8,128)(2,1)S(1)}, u32[]{:S(2)}, u32[]{:S(2)}) %collective-permute-start.25) | collective-permute-done | bytes 589856 | tf_op jit(solution)/shard_map/ppermute | solution.py:165
  415.1 4.1 collective-permute-done.31
  427.2 3.9 place.13
  431.1 3.8 place.12
  (357 shorter events, 172.6 us)
Async XLA Ops:
  1.9 28.1 %collective-permute-start = (bf16[3,192,384]{2,1,0:T(8,128)(2,1)S(1)}, bf16[3,192,384]{2,1,0:T(8,128)(2,1)}, u32[]{:S(2)}, u32[]{:S(2)}) collective-permute-start(bf16[3,192,384]{2,1,0:T(8,128)(2,1)S(1)} %constant_dynamic-slice_fusion.16), channel_id=1, source_target_pairs={{0,1},{1,0},{2,3},{3,2},{4,5},{5,4},{6,7},{7,6},{8,9},{9,8},{10,11... | collective-permute-start | bytes 1327112 | tf_op jit(solution)/shard_map/ppermute | solution.py:160
  6.9 21.0 %collective-permute-start.4 = (bf16[2304]{0:T(1024)(128)(2,1)}, bf16[2304]{0:T(1024)(128)(2,1)}, u32[]{:S(2)}, u32[]{:S(2)}) collective-permute-start(bf16[2304]{0:T(1024)(128)(2,1)} %pad_maximum_fusion.10), channel_id=1, source_target_pairs={{0,1},{1,0},{2,3},{3,2},{4,5},{5,4},{6,7},{7,6},{8,9},{9,8},{10,11... | collective-permute-start | bytes 13832 | tf_op jit(solution)/shard_map/ppermute | solution.py:160
  8.5 28.6 %collective-permute-start.5 = (bf16[96,768]{1,0:T(8,128)(2,1)}, bf16[96,768]{1,0:T(8,128)(2,1)S(1)}, u32[]{:S(2)}, u32[]{:S(2)}) collective-permute-start(bf16[96,768]{1,0:T(8,128)(2,1)} %constant_dynamic-slice_fusion.15), channel_id=1, source_target_pairs={{0,1},{1,0},{2,3},{3,2},{4,5},{5,4},{6,7},{7,6},{8,9},{9,8},{10,11... | collective-permute-start | bytes 442376 | tf_op jit(solution)/shard_map/ppermute | solution.py:160
  11.4 26.2 %collective-permute-start.9 = (bf16[192,1536]{1,0:T(8,128)(2,1)}, bf16[192,1536]{1,0:T(8,128)(2,1)}, u32[]{:S(2)}, u32[]{:S(2)}) collective-permute-start(bf16[192,1536]{1,0:T(8,128)(2,1)} %constant_dynamic-slice_fusion.14), channel_id=1, source_target_pairs={{0,1},{1,0},{2,3},{3,2},{4,5},{5,4},{6,7},{7,6},{8,9},{9,8},{10,11... | collective-permute-start | bytes 1769480 | tf_op jit(solution)/shard_map/ppermute | solution.py:160
  13.3 30.4 %collective-permute-start.13 = (bf16[384,768]{1,0:T(8,128)(2,1)}, bf16[384,768]{1,0:T(8,128)(2,1)S(1)}, u32[]{:S(2)}, u32[]{:S(2)}) collective-permute-start(bf16[384,768]{1,0:T(8,128)(2,1)} %constant_dynamic-slice_fusion.13), channel_id=1, source_target_pairs={{0,1},{1,0},{2,3},{3,2},{4,5},{5,4},{6,7},{7,6},{8,9},{9,8},{10,11... | collective-permute-start | bytes 1769480 | tf_op jit(solution)/shard_map/ppermute | solution.py:160
  30.0 27.7 %collective-permute-start.1 = (bf16[3,192,384]{2,1,0:T(8,128)(2,1)}, bf16[3,192,384]{2,1,0:T(8,128)(2,1)}, u32[]{:S(2)}, u32[]{:S(2)}) collective-permute-start(bf16[3,192,384]{2,1,0:T(8,128)(2,1)} %collective-permute-done.refs_0_), channel_id=1, source_target_pairs={{0,4},{2,6},{4,0},{6,2},{8,12},{10,14},{12,8},{14,10},{16,20},{18,... | collective-permute-start | bytes 1327112 | tf_op jit(solution)/shard_map/ppermute | solution.py:165
  37.1 20.1 %collective-permute-start.6 = (bf16[96,768]{1,0:T(8,128)(2,1)S(1)}, bf16[96,768]{1,0:T(8,128)(2,1)S(1)}, u32[]{:S(2)}, u32[]{:S(2)}) collective-permute-start(bf16[96,768]{1,0:T(8,128)(2,1)S(1)} %collective-permute-done.5.refs_0_), channel_id=1, source_target_pairs={{0,4},{2,6},{4,0},{6,2},{8,12},{10,14},{12,8},{14,10},{16,20},{18,... | collective-permute-start | bytes 442376 | tf_op jit(solution)/shard_map/ppermute | solution.py:165
  37.6 27.9 %collective-permute-start.10 = (bf16[192,1536]{1,0:T(8,128)(2,1)}, bf16[192,1536]{1,0:T(8,128)(2,1)}, u32[]{:S(2)}, u32[]{:S(2)}) collective-permute-start(bf16[192,1536]{1,0:T(8,128)(2,1)} %collective-permute-done.9.refs_0_), channel_id=1, source_target_pairs={{0,4},{2,6},{4,0},{6,2},{8,12},{10,14},{12,8},{14,10},{16,20},{18,... | collective-permute-start | bytes 1769480 | tf_op jit(solution)/shard_map/ppermute | solution.py:165
  43.7 25.6 %collective-permute-start.14 = (bf16[384,768]{1,0:T(8,128)(2,1)S(1)}, bf16[384,768]{1,0:T(8,128)(2,1)}, u32[]{:S(2)}, u32[]{:S(2)}) collective-permute-start(bf16[384,768]{1,0:T(8,128)(2,1)S(1)} %collective-permute-done.13.refs_0_), channel_id=1, source_target_pairs={{0,4},{2,6},{4,0},{6,2},{8,12},{10,14},{12,8},{14,10},{16,20},{18,... | collective-permute-start | bytes 1769480 | tf_op jit(solution)/shard_map/ppermute | solution.py:165
  64.9 37.1 %collective-permute-start.11 = (bf16[192,1536]{1,0:T(8,128)(2,1)}, bf16[192,1536]{1,0:T(8,128)(2,1)}, u32[]{:S(2)}, u32[]{:S(2)}) collective-permute-start(bf16[192,1536]{1,0:T(8,128)(2,1)} %collective-permute-done.9.refs_0_), channel_id=1, source_target_pairs={{0,2},{2,0},{4,6},{6,4},{8,10},{10,8},{12,14},{14,12},{16,18},{18,... | collective-permute-start | bytes 1769480 | tf_op jit(solution)/shard_map/ppermute | solution.py:165
  65.1 41.3 %collective-permute-start.15 = (bf16[384,768]{1,0:T(8,128)(2,1)S(1)}, bf16[384,768]{1,0:T(8,128)(2,1)}, u32[]{:S(2)}, u32[]{:S(2)}) collective-permute-start(bf16[384,768]{1,0:T(8,128)(2,1)S(1)} %collective-permute-done.13.refs_0_), channel_id=1, source_target_pairs={{0,2},{2,0},{4,6},{6,4},{8,10},{10,8},{12,14},{14,12},{16,18},{18,... | collective-permute-start | bytes 1769480 | tf_op jit(solution)/shard_map/ppermute | solution.py:165
  65.5 36.5 %collective-permute-start.12 = (bf16[192,1536]{1,0:T(8,128)(2,1)}, bf16[192,1536]{1,0:T(8,128)(2,1)}, u32[]{:S(2)}, u32[]{:S(2)}) collective-permute-start(bf16[192,1536]{1,0:T(8,128)(2,1)} %collective-permute-done.10.refs_1_), channel_id=1, source_target_pairs={{0,2},{2,0},{4,6},{6,4},{8,10},{10,8},{12,14},{14,12},{16,18},{18,... | collective-permute-start | bytes 1769480 | tf_op jit(solution)/shard_map/ppermute | solution.py:165
  69.3 37.2 %collective-permute-start.16 = (bf16[384,768]{1,0:T(8,128)(2,1)}, bf16[384,768]{1,0:T(8,128)(2,1)}, u32[]{:S(2)}, u32[]{:S(2)}) collective-permute-start(bf16[384,768]{1,0:T(8,128)(2,1)} %collective-permute-done.14.refs_1_), channel_id=1, source_target_pairs={{0,2},{2,0},{4,6},{6,4},{8,10},{10,8},{12,14},{14,12},{16,18},{18,... | collective-permute-start | bytes 1769480 | tf_op jit(solution)/shard_map/ppermute | solution.py:165
  206.5 23.7 %collective-permute-start.42 = (bf16[768,768]{1,0:T(8,128)(2,1)}, bf16[768,768]{1,0:T(8,128)(2,1)}, u32[]{:S(2)}, u32[]{:S(2)}) collective-permute-start(bf16[768,768]{1,0:T(8,128)(2,1)} %constant_dynamic-slice_fusion.4), channel_id=1, source_target_pairs={{0,2},{2,0},{4,6},{6,4},{8,10},{10,8},{12,14},{14,12},{16,18},{18,... | collective-permute-start | bytes 3538952 | tf_op jit(solution)/shard_map/ppermute | solution.py:165
  209.2 45.0 %collective-permute-start.32 = (bf16[384,1536]{1,0:T(8,128)(2,1)}, bf16[384,1536]{1,0:T(8,128)(2,1)}, u32[]{:S(2)}, u32[]{:S(2)}) collective-permute-start(bf16[384,1536]{1,0:T(8,128)(2,1)} %constant_dynamic-slice_fusion.9), channel_id=1, source_target_pairs={{0,2},{2,0},{4,6},{6,4},{8,10},{10,8},{12,14},{14,12},{16,18},{18,... | collective-permute-start | bytes 3538952 | tf_op jit(solution)/shard_map/ppermute | solution.py:165
  222.1 28.8 %collective-permute-start.44 = (bf16[768,768]{1,0:T(8,128)(2,1)S(1)}, bf16[768,768]{1,0:T(8,128)(2,1)S(1)}, u32[]{:S(2)}, u32[]{:S(2)}) collective-permute-start(bf16[768,768]{1,0:T(8,128)(2,1)S(1)} %add_convert_fusion.3), channel_id=1, source_target_pairs={{0,1},{1,0},{2,3},{3,2},{4,5},{5,4},{6,7},{7,6},{8,9},{9,8},{10,11... | collective-permute-start | bytes 3538952 | tf_op jit(solution)/shard_map/ppermute | solution.py:160
  225.1 51.0 %collective-permute-start.34 = (bf16[384,1536]{1,0:T(8,128)(2,1)S(1)}, bf16[384,1536]{1,0:T(8,128)(2,1)S(1)}, u32[]{:S(2)}, u32[]{:S(2)}) collective-permute-start(bf16[384,1536]{1,0:T(8,128)(2,1)S(1)} %add_convert_fusion.6), channel_id=1, source_target_pairs={{0,1},{1,0},{2,3},{3,2},{4,5},{5,4},{6,7},{7,6},{8,9},{9,8},{10,11... | collective-permute-start | bytes 3538952 | tf_op jit(solution)/shard_map/ppermute | solution.py:160
  228.2 51.3 %collective-permute-start.17 = (bf16[1536,384]{1,0:T(8,128)(2,1)S(1)}, bf16[1536,384]{1,0:T(8,128)(2,1)S(1)}, u32[]{:S(2)}, u32[]{:S(2)}) collective-permute-start(bf16[1536,384]{1,0:T(8,128)(2,1)S(1)} %fusion.29), channel_id=1, source_target_pairs={{0,2},{2,0},{4,6},{6,4},{8,10},{10,8},{12,14},{14,12},{16,18},{18,... | collective-permute-start | bytes 3538952 | tf_op jit(solution)/shard_map/ppermute | solution.py:165
  230.2 130.3 %collective-permute-start.28 = (f32[6912]{0:T(1024)}, f32[6912]{0:T(1024)S(1)}, u32[]{:S(2)}, u32[]{:S(2)}) collective-permute-start(f32[6912]{0:T(1024)} %add.688), channel_id=1, source_target_pairs={{0,2},{2,0},{4,6},{6,4},{8,10},{10,8},{12,14},{14,12},{16,18},{18,... | collective-permute-start | bytes 82952 | tf_op jit(solution)/shard_map/ppermute | solution.py:165
  250.9 50.1 %collective-permute-start.19 = (bf16[1536,384]{1,0:T(8,128)(2,1)S(1)}, bf16[1536,384]{1,0:T(8,128)(2,1)S(1)}, u32[]{:S(2)}, u32[]{:S(2)}) collective-permute-start(bf16[1536,384]{1,0:T(8,128)(2,1)S(1)} %add_convert_fusion.9), channel_id=1, source_target_pairs={{0,1},{1,0},{2,3},{3,2},{4,5},{5,4},{6,7},{7,6},{8,9},{9,8},{10,11... | collective-permute-start | bytes 3538952 | tf_op jit(solution)/shard_map/ppermute | solution.py:160
  254.2 50.3 %collective-permute-start.45 = (bf16[384,768]{1,0:T(8,128)(2,1)S(1)}, bf16[384,768]{1,0:T(8,128)(2,1)S(1)}, u32[]{:S(2)}, u32[]{:S(2)}) collective-permute-start(bf16[384,768]{1,0:T(8,128)(2,1)S(1)} %constant_dynamic-slice_fusion.2), channel_id=1, source_target_pairs={{0,4},{2,6},{4,0},{6,2},{8,12},{10,14},{12,8},{14,10},{16,20},{18,... | collective-permute-start | bytes 1769480 | tf_op jit(solution)/shard_map/ppermute | solution.py:165
  277.9 28.4 %collective-permute-start.35 = (bf16[192,1536]{1,0:T(8,128)(2,1)S(1)}, bf16[192,1536]{1,0:T(8,128)(2,1)S(1)}, u32[]{:S(2)}, u32[]{:S(2)}) collective-permute-start(bf16[192,1536]{1,0:T(8,128)(2,1)S(1)} %constant_dynamic-slice_fusion.7), channel_id=1, source_target_pairs={{0,4},{2,6},{4,0},{6,2},{8,12},{10,14},{12,8},{14,10},{16,20},{18,... | collective-permute-start | bytes 1769480 | tf_op jit(solution)/shard_map/ppermute | solution.py:165
  322.7 21.9 %collective-permute-start.37 = (bf16[48,1536]{1,0:T(8,128)(2,1)S(1)}, bf16[48,1536]{1,0:T(8,128)(2,1)S(1)}, u32[]{:S(2)}, u32[]{:S(2)}) collective-permute-start(bf16[48,1536]{1,0:T(8,128)(2,1)S(1)} %constant_dynamic-slice_fusion.5), channel_id=1, source_target_pairs={{0,16},{2,18},{4,20},{6,22},{8,24},{10,26},{12,28},{14,30},{16,0},... | collective-permute-start | bytes 442376 | tf_op jit(solution)/shard_map/ppermute | solution.py:165
  331.2 16.5 %collective-permute-start.22 = (bf16[192,384]{1,0:T(8,128)(2,1)S(1)}, bf16[192,384]{1,0:T(8,128)(2,1)S(1)}, u32[]{:S(2)}, u32[]{:S(2)}) collective-permute-start(bf16[192,384]{1,0:T(8,128)(2,1)S(1)} %constant_dynamic-slice_fusion.10), channel_id=1, source_target_pairs={{0,16},{2,18},{4,20},{6,22},{8,24},{10,26},{12,28},{14,30},{16,0},... | collective-permute-start | bytes 442376 | tf_op jit(solution)/shard_map/ppermute | solution.py:165
  332.7 22.9 %collective-permute-start.48 = (bf16[96,768]{1,0:T(8,128)(2,1)S(1)}, bf16[96,768]{1,0:T(8,128)(2,1)S(1)}, u32[]{:S(2)}, u32[]{:S(2)}) collective-permute-start(bf16[96,768]{1,0:T(8,128)(2,1)S(1)} %add_convert_fusion.17.refs_0_), channel_id=1, source_target_pairs={{0,16},{2,18},{4,20},{6,22},{8,24},{10,26},{12,28},{14,30},{16,0},... | collective-permute-start | bytes 442376 | tf_op jit(solution)/shard_map/ppermute | solution.py:165
  361.5 22.2 %collective-permute-start.29 = (f32[6912]{0:T(1024)S(1)}, f32[6912]{0:T(1024)S(1)}, u32[]{:S(2)}, u32[]{:S(2)}) collective-permute-start(f32[6912]{0:T(1024)S(1)} %add.689), channel_id=1, source_target_pairs={{0,4},{2,6},{4,0},{6,2},{8,12},{10,14},{12,8},{14,10},{16,20},{18,... | collective-permute-start | bytes 82952 | tf_op jit(solution)/shard_map/ppermute | solution.py:165
  363.0 16.7 %collective-permute-start.24 = (bf16[384,384]{1,0:T(8,128)(2,1)S(1)}, bf16[384,384]{1,0:T(8,128)(2,1)S(1)}, u32[]{:S(2)}, u32[]{:S(2)}) collective-permute-start(bf16[384,384]{1,0:T(8,128)(2,1)S(1)} %pad_maximum_fusion.6), channel_id=1, source_target_pairs={{0,8},{2,10},{4,12},{6,14},{8,0},{10,2},{12,4},{14,6},{16,24},{18,... | collective-permute-start | bytes 884744 | tf_op jit(solution)/shard_map/ppermute | solution.py:165
  373.6 22.6 %collective-permute-start.40 = (bf16[192,1536]{1,0:T(8,128)(2,1)S(1)}, bf16[192,1536]{1,0:T(8,128)(2,1)S(1)}, u32[]{:S(2)}, u32[]{:S(2)}) collective-permute-start(bf16[192,1536]{1,0:T(8,128)(2,1)S(1)} %pad_maximum_fusion.4), channel_id=1, source_target_pairs={{0,4},{2,6},{4,0},{6,2},{8,12},{10,14},{12,8},{14,10},{16,20},{18,... | collective-permute-start | bytes 1769480 | tf_op jit(solution)/shard_map/ppermute | solution.py:165
  379.8 27.9 %collective-permute-start.25 = (bf16[768,384]{1,0:T(8,128)(2,1)S(1)}, bf16[768,384]{1,0:T(8,128)(2,1)S(1)}, u32[]{:S(2)}, u32[]{:S(2)}) collective-permute-start(bf16[768,384]{1,0:T(8,128)(2,1)S(1)} %pad_maximum_fusion.3), channel_id=1, source_target_pairs={{0,4},{2,6},{4,0},{6,2},{8,12},{10,14},{12,8},{14,10},{16,20},{18,... | collective-permute-start | bytes 1769480 | tf_op jit(solution)/shard_map/ppermute | solution.py:165
  383.7 30.7 %collective-permute-start.30 = (f32[6912]{0:T(1024)S(1)}, f32[6912]{0:T(1024)S(1)}, u32[]{:S(2)}, u32[]{:S(2)}) collective-permute-start(f32[6912]{0:T(1024)S(1)} %add.690), channel_id=1, source_target_pairs={{0,8},{2,10},{4,12},{6,14},{8,0},{10,2},{12,4},{14,6},{16,24},{18,... | collective-permute-start | bytes 82952 | tf_op jit(solution)/shard_map/ppermute | solution.py:165
  384.9 41.1 %collective-permute-start.51 = (bf16[768,768]{1,0:T(8,128)(2,1)}, bf16[768,768]{1,0:T(8,128)(2,1)}, u32[]{:S(2)}, u32[]{:S(2)}) collective-permute-start(bf16[768,768]{1,0:T(8,128)(2,1)} %pad_maximum_fusion.2), channel_id=1, source_target_pairs={{0,2},{2,0},{4,6},{6,4},{8,10},{10,8},{12,14},{14,12},{16,18},{18,... | collective-permute-start | bytes 3538952 | tf_op jit(solution)/shard_map/ppermute | solution.py:165
  397.4 33.8 %collective-permute-start.41 = (bf16[384,1536]{1,0:T(8,128)(2,1)}, bf16[384,1536]{1,0:T(8,128)(2,1)}, u32[]{:S(2)}, u32[]{:S(2)}) collective-permute-start(bf16[384,1536]{1,0:T(8,128)(2,1)} %pad_maximum_fusion.1), channel_id=1, source_target_pairs={{0,2},{2,0},{4,6},{6,4},{8,10},{10,8},{12,14},{14,12},{16,18},{18,... | collective-permute-start | bytes 3538952 | tf_op jit(solution)/shard_map/ppermute | solution.py:165
  (86 other events, 987.5 us)
